TPU v7x, 256 devices: a whole 4x4x8 slice. The times are simulated.
256 devices in a mesh: wide: 64 (over x, y, z_lo, core), pol: 4 (over z_hi).
Axes of the slice: x: 4, y: 4, z: 8 (z_hi: 4, z_lo: 2; z = z_hi * 2 + z_lo), core: 2. Of those that a mesh axis runs over, the one named last changes fastest.
Arguments:
- voltages: bfloat16 [2, 4, 1024, 128, 256], P(None, 'pol', 'wide'), may hold values from -6 to 6
- gains: float32 [2, 2, 1024, 128], P(None, None, 'wide'), may hold values from -0.04 to 0.04
- cylinder_feed_lookup: int32 [1024], replicated, may hold values from 0 to 1023, each once
- beam_bins: int32 [128, 256], P('wide'), may hold values from 0 to 511
Outputs:
- intensity: float32 [1024, 128, 256], P(('wide', 'pol'))
Inputs may be any that keep to these rules, and one draw needn't show every extreme that they name: `cylinder_feed_lookup`: every feed of 0 to 1023 appears once.
All inputs are finite; a program needn't handle non-finite values.
Results may differ from a plain program's by a relative error of at most 0.0024.
Values may be sent and summed in bfloat16 or wider, within the bound.
No kernel may reach another device: no remote copies, remote signals or barrier semaphores. Data moves between devices by JAX's collectives and lax.ppermute only.
A program may use at most 64 MiB of HBM per device.

v0:
```python
import itertools
import math

import jax
import jax.numpy as jnp
from jax import lax
from jax.experimental import pallas as pl
from jax.experimental.pallas import tpu as pltpu
from jax.sharding import PartitionSpec as P

MEGA = 2**20


def owner_slot(owner):
    x, y, z, core, stream = owner // 64, owner // 16 % 4, owner // 8 % 2, owner // 4 % 2, owner % 4
    return (stream * 2 + z) * 32 + (x * 4 + y) * 2 + core


def corner_slot(device):
    x, y, z, core = device // 16, device // 4 % 4, device // 2 % 2, device % 2
    return x * 16 + z * 8 + core * 4 + y


def dft_table(bins, feeds_per):
    along = lax.iota(jnp.int32, feeds_per)
    product = bins[:, :, None] * along[None, None, :] % (2 * feeds_per)
    theta = product.astype(jnp.float32) * (math.pi / feeds_per)
    cos_table = jnp.cos(theta).astype(jnp.bfloat16)
    sin_table = jnp.sin(theta).astype(jnp.bfloat16)
    return jnp.concatenate([cos_table, sin_table], axis=1)


def calibrate_kernel(volts_ref, gains_ref, out_ref, in_buf, gain_buf, out_buf, in_sem, gain_sem, out_sem):
    chunks, _, feeds, block, samples = in_buf.shape

    def fetch(i):
        own = volts_ref.at[:, 0, :, pl.ds(i * block, block), :]
        return pltpu.make_async_copy(own, in_buf.at[i], in_sem.at[i])

    def store(i):
        own = out_ref.at[pl.ds(i * block // 2, block // 2)]
        return pltpu.make_async_copy(out_buf.at[i], own, out_sem.at[i])

    gain_copy = pltpu.make_async_copy(gains_ref, gain_buf, gain_sem)
    gain_copy.start()
    for i in range(chunks):
        fetch(i).start()
    row = lax.broadcasted_iota(jnp.int32, (feeds * 16, feeds * 16), 0)
    col = lax.broadcasted_iota(jnp.int32, (feeds * 16, feeds * 16), 1)
    swap = (row // feeds == col % 16) & (row % feeds == col // 16)
    swap = swap.astype(jnp.float32).astype(jnp.bfloat16)
    gain_copy.wait()
    polar = lax.axis_index("pol") // 2
    gain_real = gain_buf[0, polar]
    gain_imag = gain_buf[1, polar]
    for i in range(chunks):
        fetch(i).wait()
        for group in range(block // 16):
            parts = []
            for part in range(2):
                own = in_buf[i, part, :, group * 16 : group * 16 + 16, :].reshape(feeds * 16, samples)
                parts.append(jnp.dot(swap, own, preferred_element_type=jnp.float32))
            for c in range(16):
                at = group * 16 + c
                channel = i * block + at
                own_real = gain_real[:, channel : channel + 1]
                own_imag = gain_imag[:, channel : channel + 1]
                volt_real = parts[0][c * feeds : c * feeds + feeds]
                volt_imag = parts[1][c * feeds : c * feeds + feeds]
                cal_real = own_real * volt_real - own_imag * volt_imag
                cal_imag = own_real * volt_imag + own_imag * volt_real
                out_buf[i, corner_slot(channel // 2) - i * block // 2, at % 2, 0] = cal_real.astype(jnp.bfloat16)
                out_buf[i, corner_slot(channel // 2) - i * block // 2, at % 2, 1] = cal_imag.astype(jnp.bfloat16)
        store(i).start()
    for i in range(chunks):
        store(i).wait()


def calibrate(voltages, gains):
    _, _, feeds, channels, samples = voltages.shape
    chunks = 2
    block = channels // chunks
    return pl.pallas_call(
        calibrate_kernel,
        out_shape=jax.ShapeDtypeStruct((channels // 2, 2, 2, feeds, samples), jnp.bfloat16),
        in_specs=[pl.BlockSpec(memory_space=pl.ANY)] * 2,
        out_specs=pl.BlockSpec(memory_space=pl.ANY),
        scratch_shapes=[
            pltpu.VMEM((chunks, 2, feeds, block, samples), jnp.bfloat16),
            pltpu.VMEM(gains.shape, jnp.float32),
            pltpu.VMEM((chunks, block // 2, 2, 2, feeds, samples), jnp.bfloat16),
            pltpu.SemaphoreType.DMA((chunks,)),
            pltpu.SemaphoreType.DMA,
            pltpu.SemaphoreType.DMA((chunks,)),
        ],
        compiler_params=pltpu.CompilerParams(vmem_limit_bytes=60 * MEGA),
        cost_estimate=pl.CostEstimate(flops=2**29, bytes_accessed=4 * MEGA, transcendentals=0),
        name="calibrate",
    )(voltages, gains)


def beam_powers(real_parts, imag_parts):
    sum_re, sum_im = real_parts[0] + real_parts[2], imag_parts[0] + imag_parts[2]
    dif_re, dif_im = real_parts[0] - real_parts[2], imag_parts[0] - imag_parts[2]
    odd_re, odd_im = real_parts[1] + real_parts[3], imag_parts[1] + imag_parts[3]
    odd_dif_re, odd_dif_im = real_parts[1] - real_parts[3], imag_parts[1] - imag_parts[3]
    each = [
        (sum_re + odd_re, sum_im + odd_im),
        (dif_re + odd_dif_im, dif_im - odd_dif_re),
        (sum_re - odd_re, sum_im - odd_im),
        (dif_re - odd_dif_im, dif_im + odd_dif_re),
    ]
    return [a * a + b * b for a, b in each]


def one_hot(hit):
    return hit.astype(jnp.float32).astype(jnp.bfloat16)


def route_kernel(rows_ref, lookup_ref, table_ref, swap_ref, choice_ref, first_ref, second_ref, second_buf, sem):
    groups, size = rows_ref.shape
    column = lax.broadcasted_iota(jnp.int32, (size, 128), 0)
    lane = lax.broadcasted_iota(jnp.int32, (size, 128), 1)
    block = [rows_ref[c : c + 1] >> 8 for c in range(groups)]
    rank, left = [], [[None] * groups for _ in range(groups)]
    for c in range(groups):
        own = lookup_ref[pl.ds(c * size, size)] >> 8
        parts = []
        for at in range(0, size, 128):
            before = (own == block[c][:, at : at + 128]) & (column < lane + at)
            parts.append(jnp.sum(before.astype(jnp.int32), axis=0, keepdims=True))
        rank.append(jnp.concatenate(parts, axis=1))
        for b in range(groups):
            left[b][c] = jnp.sum((block[c] == b).astype(jnp.int32))
    used = [[0] * groups for _ in range(groups)]
    place = [jnp.zeros((1, size), jnp.int32) for _ in range(groups)]
    choice = [jnp.zeros((size, 128), jnp.int32) for _ in range(groups)]
    start = 0
    for target in itertools.permutations(range(groups)):
        weight = left[0][target[0]]
        for b in range(1, groups):
            weight = jnp.minimum(weight, left[b][target[b]])
        inside = (column >= start) & (column < start + weight)
        for b in range(groups):
            c = target[b]
            low = used[b][c]
            hit = (block[c] == b) & (rank[c] >= low) & (rank[c] < low + weight)
            place[c] = jnp.where(hit, rank[c] + (start - low), place[c])
            choice[c] = jnp.where(inside, b, choice[c])
            left[b][c] = left[b][c] - weight
            used[b][c] = low + weight
        start = start + weight
    down = lax.broadcasted_iota(jnp.int32, (size, size), 0)
    across = lax.broadcasted_iota(jnp.int32, (size, size), 1)
    code = choice[0]
    for c in range(1, groups):
        code = code + choice[c] * 4**c
    choice_ref[...] = code
    upright = [jnp.sum(jnp.where(down == across, place[c], 0), axis=1, keepdims=True) for c in range(groups)]
    store = pltpu.make_async_copy(second_buf, second_ref.at[0], sem)
    for channel, own_ref in ((1, second_buf), (0, first_ref)):
        for c in range(groups):
            order = one_hot(upright[c] == across)
            own = jnp.dot(table_ref[channel], order, preferred_element_type=jnp.float32)
            own_ref[c] = own.astype(jnp.bfloat16)
        if channel == 1:
            store.start()
    for b in range(groups):
        for at in range(0, size, 128):
            total = jnp.zeros((1, 128), jnp.int32)
            for c in range(groups):
                hit = lookup_ref[pl.ds(c * size, size)] == lane + (b * size + at)
                total += jnp.sum(jnp.where(hit, upright[c], 0), axis=0, keepdims=True)
            swap_ref[pl.ds(b, 1), pl.ds(at, 128)] = total
    store.wait()


def route(rows, lookup, table):
    groups, size = rows.shape
    _, twice, _ = table.shape
    return pl.pallas_call(
        route_kernel,
        out_shape=(
            jax.ShapeDtypeStruct((groups, size), jnp.int32),
            jax.ShapeDtypeStruct((size, 128), jnp.int32),
            jax.ShapeDtypeStruct((groups, twice, size), jnp.bfloat16),
            jax.ShapeDtypeStruct((12, groups, twice, size), jnp.bfloat16),
        ),
        in_specs=[pl.BlockSpec(memory_space=pltpu.VMEM)] * 3,
        out_specs=(pl.BlockSpec(memory_space=pltpu.VMEM),) * 3 + (pl.BlockSpec(memory_space=pl.ANY),),
        scratch_shapes=[pltpu.VMEM((groups, twice, size), jnp.bfloat16), pltpu.SemaphoreType.DMA],
        compiler_params=pltpu.CompilerParams(vmem_limit_bytes=44 * MEGA),
        cost_estimate=pl.CostEstimate(flops=2 * 2**30, bytes_accessed=8 * MEGA, transcendentals=0),
        name="route",
    )(rows, lookup, table)


def beams_kernel(turned_ref, swap_ref, choice_ref, first_ref, second_ref, out_ref, grid_ref, second_buf, sem):
    sources, channels, _, feeds, samples = turned_ref.shape
    feeds_total = sources * feeds
    cylinders, size = swap_ref.shape
    fetch = pltpu.make_async_copy(second_ref.at[0], second_buf, sem)
    fetch.start()
    down = lax.broadcasted_iota(jnp.int32, (size, size), 0)
    swap = [one_hot(swap_ref[b : b + 1] == down) for b in range(cylinders)]
    def swaps(channel):
        for part in range(2):
            own = turned_ref[:, channel, part].reshape(feeds_total, samples)
            moved = [
                jnp.dot(swap[b], own[b * size : b * size + size], preferred_element_type=jnp.float32)
                for b in range(cylinders)
            ]
            for at in range(0, samples, 128):
                for c in range(cylinders):
                    pick = (choice_ref[...] >> (2 * c)) & 3
                    got = moved[3][:, at : at + 128]
                    for b in range(3):
                        got = jnp.where(pick == b, moved[b][:, at : at + 128], got)
                    grid_ref[channel, c, part, :, pl.ds(at, 128)] = got.astype(jnp.bfloat16)

    def field_of(channel, table_ref, c):
        by_real, by_imag = [
            jnp.dot(table_ref[c], grid_ref[channel, c, part], preferred_element_type=jnp.float32)
            for part in range(2)
        ]
        return by_real[:size] + by_imag[size:], by_imag[:size] - by_real[size:]

    def powers(channel, field, rows):
        for row in rows:
            halves = []
            for at in range(0, samples, 128):
                re = [field[c][0][row : row + 8, at : at + 128] for c in range(cylinders)]
                im = [field[c][1][row : row + 8, at : at + 128] for c in range(cylinders)]
                halves.append(beam_powers(re, im))
            for e in range(cylinders):
                low = jnp.concatenate([halves[0][e][:4], halves[1][e][:4]], axis=0)
                high = jnp.concatenate([halves[0][e][4:], halves[1][e][4:]], axis=0)
                at = e * (size // 4) + row // 4
                out_ref[owner_slot(at), pl.ds(channel * 8, 8)] = low.astype(jnp.bfloat16)
                out_ref[owner_slot(at + 1), pl.ds(channel * 8, 8)] = high.astype(jnp.bfloat16)

    swaps(0)
    zero = [field_of(0, first_ref, c) for c in range(cylinders)]
    swaps(1)
    powers(0, zero, range(0, size // 2, 8))
    fetch.wait()
    one = []
    for c in range(cylinders):
        one.append(field_of(1, second_buf, c))
        powers(0, zero, range(size // 2 + c * size // 8, size // 2 + (c + 1) * size // 8, 8))
    powers(1, one, range(0, size, 8))


def form_beams(turned, swap, choice, first, second):
    sources, channels, _, feeds, samples = turned.shape
    feeds_total = sources * feeds
    return pl.pallas_call(
        beams_kernel,
        out_shape=jax.ShapeDtypeStruct((feeds_total // 4, 16, 128), jnp.bfloat16),
        in_specs=[pl.BlockSpec(memory_space=pltpu.VMEM)] * 4 + [pl.BlockSpec(memory_space=pl.ANY)],
        out_specs=pl.BlockSpec(memory_space=pltpu.VMEM),
        scratch_shapes=[
            pltpu.VMEM((channels, 4, 2, feeds_total // 4, samples), jnp.bfloat16),
            pltpu.VMEM(first.shape, jnp.bfloat16),
            pltpu.SemaphoreType.DMA,
        ],
        compiler_params=pltpu.CompilerParams(vmem_limit_bytes=44 * MEGA),
        cost_estimate=pl.CostEstimate(flops=3 * 2**29, bytes_accessed=8 * MEGA, transcendentals=0),
        name="form_beams",
    )(turned, swap, choice, first, second)


def total_kernel(sent_ref, out_ref, total_ref, out_buf, out_sem):
    chunks = out_sem.shape[0]
    block = total_ref.shape[0] // 16 // chunks

    def store(i):
        own = pl.ds(i * 2 * block, 2 * block)
        return pltpu.make_async_copy(out_buf.at[:, own], out_ref.at[:, own], out_sem.at[i])

    for i in range(chunks):
        for source in range(i * block, i * block + block):
            own = [sent_ref[owner_slot(source * 4 + stream)].astype(jnp.float32) for stream in range(4)]
            total_ref[pl.ds(source * 16, 16)] = (own[0] + own[1]) + (own[2] + own[3])
        for beam in range(4):
            for half in range(2):
                rows = total_ref[pl.ds(i * block * 16 + half * 4 + beam, 2 * block, stride=8)]
                out_buf[beam, pl.ds(i * 2 * block, 2 * block), pl.ds(half * 128, 128)] = rows
        store(i).start()
    for i in range(chunks):
        store(i).wait()


def add_streams(sent):
    blocks = sent.shape[0] // 4
    chunks = 4
    return pl.pallas_call(
        total_kernel,
        out_shape=jax.ShapeDtypeStruct((4, 2 * blocks, 256), jnp.float32),
        in_specs=[pl.BlockSpec(memory_space=pltpu.VMEM)],
        out_specs=pl.BlockSpec(memory_space=pl.ANY),
        scratch_shapes=[
            pltpu.VMEM((blocks * 16, 128), jnp.float32),
            pltpu.VMEM((4, 2 * blocks, 256), jnp.float32),
            pltpu.SemaphoreType.DMA((chunks,)),
        ],
        compiler_params=pltpu.CompilerParams(vmem_limit_bytes=16 * MEGA),
        cost_estimate=pl.CostEstimate(flops=2**20, bytes_accessed=2 * MEGA, transcendentals=0),
        name="add_streams",
    )(sent)


def body(voltages, gains, cylinder_feed_lookup, beam_bins):
    calibrated = calibrate(voltages, gains)
    devices = calibrated.shape[0]
    order = sorted(range(devices), key=corner_slot)
    turned = lax.all_to_all(
        calibrated, "wide", split_axis=0, concat_axis=0, axis_index_groups=[order], tiled=True
    )
    cylinder_feed_lookup = corner_slot(cylinder_feed_lookup // 16) * 16 + cylinder_feed_lookup % 16
    lookup = jnp.broadcast_to(cylinder_feed_lookup[:, None], (cylinder_feed_lookup.shape[0], 128))
    table = dft_table(beam_bins, beam_bins.shape[1])
    swap, choice, first, second = route(cylinder_feed_lookup.reshape(4, -1), lookup, table)
    power = form_beams(turned, swap, choice, first, second)
    owners = power.shape[0]
    order = sorted(range(owners), key=owner_slot)
    sent = lax.all_to_all(
        power, ("wide", "pol"), split_axis=0, concat_axis=0, axis_index_groups=[order], tiled=True
    )
    return add_streams(sent)


def solution(mesh):
    return jax.shard_map(
        body,
        mesh=mesh,
        in_specs=(
            P(None, "pol", "wide", None, None),
            P(None, None, "wide", None),
            P(),
            P("wide", None),
        ),
        out_specs=P(("wide", "pol"), None, None),
        check_vma=False,
    )
```

profile of v0, /device:TPU:1, one launch (start us, length us, event | category | flops | bytes accessed | tf_op | source)
XLA Modules:
  0.0 86.9 jit_solution(9636042895096962027)
XLA Ops:
  0.0 3.2 %calibrate.1 = bf16[64,2,2,16,256]{4,3,2,1,0:T(8,128)(2,1)} custom-call(bf16[2,1,16,128,256]{4,3,2,1,0:T(8,128)(2,1)} %volts_ref.1, f32[2,2,16,128]{3,2,1,0:T(8,128)} %gains_ref.1), custom_call_target="tpu_custom_call" | custom-call | flops 536870912 | bytes 4194304 | tf_op jit(solution)/shard_map/calibrate/pallas_call | solution.py:83
  3.2 0.0 copy-start
  3.2 0.0 copy-start.1
  3.2 10.4 %all-to-all-start = ((bf16[64,2,2,16,256]{4,3,2,1,0:T(8,128)(2,1)}), bf16[64,2,2,16,256]{4,3,2,1,0:T(8,128)(2,1)S(1)}, u32[]{:S(2)}, u32[]{:S(2)}) async-start(bf16[64,2,2,16,256]{4,3,2,1,0:T(8,128)(2,1)} %calibrate.1), calls=%async_computation | async-start | bytes 4194304 | tf_op jit(solution)/shard_map/all_to_all | solution.py:317
  13.6 0.0 copy-done
  13.7 0.0 copy-done.1
  13.7 2.5 %cosine_convert_fusion = (bf16[2,256,256]{2,1,0:T(8,128)(2,1)S(1)}, bf16[2,256,256]{2,1,0:T(8,128)(2,1)S(1)}) fusion(s32[2,256]{1,0:T(2,128)S(1)} %copy-done.1), kind=kLoop, calls=%fused_computation.8 | loop fusion | flops 2097152 | bytes 526336 | tf_op jit(solution)/shard_map/convert_element_type | solution.py:28
  16.2 0.2 broadcast_in_dim.2.lookup_ref
  16.4 4.3 %route.1 = (s32[4,256]{1,0:T(4,128)S(1)}, s32[256,128]{1,0:T(8,128)S(1)}, bf16[4,512,256]{2,1,0:T(8,128)(2,1)S(1)}, bf16[12,4,512,256]{3,2,1,0:T(8,128)(2,1)}) custom-call(s32[4,256]{1,0:T(4,128)S(1)} %reshape.5.rows_ref, s32[1024,128]{1,0:T(8,128)S(1)} %broadcast_in_dim.2.lookup_ref, bf16[2,512,256]{2,1,0:T(8,128)(2,1)S(1)} %pad_maximum_fusion.table_ref), custom_call_target="tpu_custom_call" | custom-call | flops 2147483648 | bytes 8388608 | tf_op jit(solution)/shard_map/route/pallas_call | solution.py:181
  20.7 20.4 %all-to-all-done.turned_ref = bf16[64,2,2,16,256]{4,3,2,1,0:T(8,128)(2,1)S(1)} async-done(((bf16[64,2,2,16,256]{4,3,2,1,0:T(8,128)(2,1)}), bf16[64,2,2,16,256]{4,3,2,1,0:T(8,128)(2,1)S(1)}, u32[]{:S(2)}, u32[]{:S(2)}) %all-to-all-start) | async-done | bytes 2097184 | tf_op jit(solution)/shard_map/all_to_all | solution.py:317
  41.2 2.9 %form_beams.1 = bf16[256,16,128]{2,1,0:T(8,128)(2,1)S(1)} custom-call(bf16[64,2,2,16,256]{4,3,2,1,0:T(8,128)(2,1)S(1)} %all-to-all-done.turned_ref, s32[4,256]{1,0:T(4,128)S(1)} %get-tuple-element.9.swap_ref, s32[256,128]{1,0:T(8,128)S(1)} %get-tuple-element.10.choice_ref, bf16[4,512,256]{2,1,0:T(8,128)(2,1)S(1)} %get-tuple-element.11.first_ref, ...), custom_call_target="tpu_custom_call" | custom-call | flops 1610612736 | bytes 8388608 | tf_op jit(solution)/shard_map/form_beams/pallas_call | solution.py:257
  44.1 41.9 %all_to_all.10.sent_ref = bf16[256,16,128]{2,1,0:T(8,128)(2,1)S(1)} all-to-all(bf16[256,16,128]{2,1,0:T(8,128)(2,1)S(1)} %form_beams.1), channel_id=1, replica_groups={{0,4,16,20,32,36,48,52,64,68,80,84,96,100,112,116,128,132,144,148,160,1..., dimensions={0} | all-to-all | bytes 2097152 | tf_op jit(solution)/shard_map/all_to_all | solution.py:327
  86.0 0.9 add_streams.1
  (3 shorter events, 0.1 us)
Async XLA Ops:
  3.2 10.4 %copy-start = (s32[1024]{0:T(1024)S(1)}, s32[1024]{0:T(1024)}, u32[]{:S(2)}) copy-start(s32[1024]{0:T(1024)} %param.6) | copy-start | bytes 12292
  3.2 10.4 %copy-start.1 = (s32[2,256]{1,0:T(2,128)S(1)}, s32[2,256]{1,0:T(2,128)}, u32[]{:S(2)}) copy-start(s32[2,256]{1,0:T(2,128)} %param.7) | copy-start | bytes 6148
  3.2 37.9 %all-to-all-start = ((bf16[64,2,2,16,256]{4,3,2,1,0:T(8,128)(2,1)}), bf16[64,2,2,16,256]{4,3,2,1,0:T(8,128)(2,1)S(1)}, u32[]{:S(2)}, u32[]{:S(2)}) async-start(bf16[64,2,2,16,256]{4,3,2,1,0:T(8,128)(2,1)} %calibrate.1), calls=%async_computation | async-start | bytes 4194304 | tf_op jit(solution)/shard_map/all_to_all | solution.py:317
where the time goes:
time: 87.2 us; the launch traced here: 86.9 us
  blocking collectives  41.9 us (48%)
  waiting for transfers between devices  20.4 us (23%)
  Pallas kernels  11.3 us (13%)
  starting transfers between devices  10.4 us (12%)
  other arithmetic  2.56 us (3%)
    all_to_all x1, blocking collectives, body(): lax.all_to_all(power, ('wide', 'pol'), split_axis=0, concat_axis=0, axis_...  41.9 us
    all_to_all x1, waiting for transfers between devices, body(): lax.all_to_all(calibrated, 'wide', split_axis=0, concat_axis=0, axis_inde...  20.4 us
    all_to_all x1, starting transfers between devices, body(): lax.all_to_all(calibrated, 'wide', split_axis=0, concat_axis=0, axis_inde...  10.4 us
    pallas_call x1, Pallas kernels, route(): pl.pallas_call(route_kernel, out_shape=(jax.ShapeDtypeStruct((groups, siz...  4.32 us
    pallas_call x1, Pallas kernels, calibrate(): pl.pallas_call(calibrate_kernel, out_shape=jax.ShapeDtypeStruct((channels...  3.21 us
    pallas_call x1, Pallas kernels, form_beams(): pl.pallas_call(beams_kernel, out_shape=jax.ShapeDtypeStruct((feeds_total...  2.92 us
    convert_element_type x1, other arithmetic, dft_table(): cos_table = jnp.cos(theta).astype(jnp.bfloat16)  2.5 us
  transfers between devices with their start and end apart: 1, of which 1 were waited for; matrix products, arithmetic and copies ran while one was open for 3% of the time, Pallas kernels for 5%

commit v1 on v0

--- a/solution.py
+++ b/solution.py
@@ -18,7 +18,7 @@
 
 def corner_slot(device):
     x, y, z, core = device // 16, device // 4 % 4, device // 2 % 2, device % 2
-    return x * 16 + z * 8 + core * 4 + y
+    return x * 16 + core * 8 + z * 4 + y
 
 
 def dft_table(bins, feeds_per):

time: 87.2 us -> 86.9 us (level)
  blocking collectives: 41.9 us -> 40.8 us
  waiting for transfers between devices: 20.4 us -> 21.4 us
    all_to_all x1, blocking collectives: 41.9 us -> 40.8 us  [body(): lax.all_to_all(power, ('wide', 'pol'), split_axis=0, concat_axis=0, axis_...]
    all_to_all x1, waiting for transfers between devices: 20.4 us -> 21.4 us  [body(): lax.all_to_all(calibrated, 'wide', split_axis=0, concat_axis=0, axis_inde...]
where the time goes in v1:
time: 86.9 us; the launch traced here: 86.7 us
  blocking collectives  40.8 us (47%)
  waiting for transfers between devices  21.4 us (25%)
  Pallas kernels  11.3 us (13%)
  starting transfers between devices  10.4 us (12%)
  other arithmetic  2.56 us (3%)
    all_to_all x1, blocking collectives, body(): lax.all_to_all(power, ('wide', 'pol'), split_axis=0, concat_axis=0, axis_...  40.8 us
    all_to_all x1, waiting for transfers between devices, body(): lax.all_to_all(calibrated, 'wide', split_axis=0, concat_axis=0, axis_inde...  21.4 us
    all_to_all x1, starting transfers between devices, body(): lax.all_to_all(calibrated, 'wide', split_axis=0, concat_axis=0, axis_inde...  10.4 us
    pallas_call x1, Pallas kernels, route(): pl.pallas_call(route_kernel, out_shape=(jax.ShapeDtypeStruct((groups, siz...  4.32 us
    pallas_call x1, Pallas kernels, calibrate(): pl.pallas_call(calibrate_kernel, out_shape=jax.ShapeDtypeStruct((channels...  3.21 us
    pallas_call x1, Pallas kernels, form_beams(): pl.pallas_call(beams_kernel, out_shape=jax.ShapeDtypeStruct((feeds_total...  2.92 us
    convert_element_type x1, other arithmetic, dft_table(): cos_table = jnp.cos(theta).astype(jnp.bfloat16)  2.5 us
  transfers between devices with their start and end apart: 1, of which 1 were waited for; matrix products, arithmetic and copies ran while one was open for 3% of the time, Pallas kernels for 5%

profile of v1, /device:TPU:1, one launch (start us, length us, event | category | flops | bytes accessed | tf_op | source)
XLA Modules:
  0.0 86.7 jit_solution(14232351274495913747)
XLA Ops:
  0.0 3.2 %calibrate.1 = bf16[64,2,2,16,256]{4,3,2,1,0:T(8,128)(2,1)} custom-call(bf16[2,1,16,128,256]{4,3,2,1,0:T(8,128)(2,1)} %volts_ref.1, f32[2,2,16,128]{3,2,1,0:T(8,128)} %gains_ref.1), custom_call_target="tpu_custom_call" | custom-call | flops 536870912 | bytes 4194304 | tf_op jit(solution)/shard_map/calibrate/pallas_call | solution.py:83
  3.2 0.0 copy-start
  3.2 0.0 copy-start.1
  3.2 10.4 %all-to-all-start = ((bf16[64,2,2,16,256]{4,3,2,1,0:T(8,128)(2,1)}), bf16[64,2,2,16,256]{4,3,2,1,0:T(8,128)(2,1)S(1)}, u32[]{:S(2)}, u32[]{:S(2)}) async-start(bf16[64,2,2,16,256]{4,3,2,1,0:T(8,128)(2,1)} %calibrate.1), calls=%async_computation | async-start | bytes 4194304 | tf_op jit(solution)/shard_map/all_to_all | solution.py:317
  13.6 0.0 copy-done
  13.7 0.0 copy-done.1
  13.7 2.5 %cosine_convert_fusion = (bf16[2,256,256]{2,1,0:T(8,128)(2,1)S(1)}, bf16[2,256,256]{2,1,0:T(8,128)(2,1)S(1)}) fusion(s32[2,256]{1,0:T(2,128)S(1)} %copy-done.1), kind=kLoop, calls=%fused_computation.8 | loop fusion | flops 2097152 | bytes 526336 | tf_op jit(solution)/shard_map/convert_element_type | solution.py:28
  16.2 0.2 broadcast_in_dim.2.lookup_ref
  16.4 4.3 %route.1 = (s32[4,256]{1,0:T(4,128)S(1)}, s32[256,128]{1,0:T(8,128)S(1)}, bf16[4,512,256]{2,1,0:T(8,128)(2,1)S(1)}, bf16[12,4,512,256]{3,2,1,0:T(8,128)(2,1)}) custom-call(s32[4,256]{1,0:T(4,128)S(1)} %reshape.5.rows_ref, s32[1024,128]{1,0:T(8,128)S(1)} %broadcast_in_dim.2.lookup_ref, bf16[2,512,256]{2,1,0:T(8,128)(2,1)S(1)} %pad_maximum_fusion.table_ref), custom_call_target="tpu_custom_call" | custom-call | flops 2147483648 | bytes 8388608 | tf_op jit(solution)/shard_map/route/pallas_call | solution.py:181
  20.7 21.4 %all-to-all-done.turned_ref = bf16[64,2,2,16,256]{4,3,2,1,0:T(8,128)(2,1)S(1)} async-done(((bf16[64,2,2,16,256]{4,3,2,1,0:T(8,128)(2,1)}), bf16[64,2,2,16,256]{4,3,2,1,0:T(8,128)(2,1)S(1)}, u32[]{:S(2)}, u32[]{:S(2)}) %all-to-all-start) | async-done | bytes 2097184 | tf_op jit(solution)/shard_map/all_to_all | solution.py:317
  42.1 2.9 %form_beams.1 = bf16[256,16,128]{2,1,0:T(8,128)(2,1)S(1)} custom-call(bf16[64,2,2,16,256]{4,3,2,1,0:T(8,128)(2,1)S(1)} %all-to-all-done.turned_ref, s32[4,256]{1,0:T(4,128)S(1)} %get-tuple-element.9.swap_ref, s32[256,128]{1,0:T(8,128)S(1)} %get-tuple-element.10.choice_ref, bf16[4,512,256]{2,1,0:T(8,128)(2,1)S(1)} %get-tuple-element.11.first_ref, ...), custom_call_target="tpu_custom_call" | custom-call | flops 1610612736 | bytes 8388608 | tf_op jit(solution)/shard_map/form_beams/pallas_call | solution.py:257
  45.0 40.8 %all_to_all.10.sent_ref = bf16[256,16,128]{2,1,0:T(8,128)(2,1)S(1)} all-to-all(bf16[256,16,128]{2,1,0:T(8,128)(2,1)S(1)} %form_beams.1), channel_id=1, replica_groups={{0,4,16,20,32,36,48,52,64,68,80,84,96,100,112,116,128,132,144,148,160,1..., dimensions={0} | all-to-all | bytes 2097152 | tf_op jit(solution)/shard_map/all_to_all | solution.py:327
  85.8 0.9 %add_streams.1 = f32[4,128,256]{2,1,0:T(8,128)} custom-call(bf16[256,16,128]{2,1,0:T(8,128)(2,1)S(1)} %all_to_all.10.sent_ref), custom_call_target="tpu_custom_call" | custom-call | flops 1048576 | bytes 2097152 | tf_op jit(solution)/shard_map/add_streams/pallas_call | solution.py:297
  (3 shorter events, 0.1 us)
Async XLA Ops:
  3.2 10.4 %copy-start = (s32[1024]{0:T(1024)S(1)}, s32[1024]{0:T(1024)}, u32[]{:S(2)}) copy-start(s32[1024]{0:T(1024)} %param.6) | copy-start | bytes 12292
  3.2 10.4 %copy-start.1 = (s32[2,256]{1,0:T(2,128)S(1)}, s32[2,256]{1,0:T(2,128)}, u32[]{:S(2)}) copy-start(s32[2,256]{1,0:T(2,128)} %param.7) | copy-start | bytes 6148
  3.2 38.9 %all-to-all-start = ((bf16[64,2,2,16,256]{4,3,2,1,0:T(8,128)(2,1)}), bf16[64,2,2,16,256]{4,3,2,1,0:T(8,128)(2,1)S(1)}, u32[]{:S(2)}, u32[]{:S(2)}) async-start(bf16[64,2,2,16,256]{4,3,2,1,0:T(8,128)(2,1)} %calibrate.1), calls=%async_computation | async-start | bytes 4194304 | tf_op jit(solution)/shard_map/all_to_all | solution.py:317

commit v2 on v1

--- a/solution.py
+++ b/solution.py
@@ -18,7 +18,7 @@
 
 def corner_slot(device):
     x, y, z, core = device // 16, device // 4 % 4, device // 2 % 2, device % 2
-    return x * 16 + core * 8 + z * 4 + y
+    return x * 16 + core * 8 + z * 4 + 3 - y
 
 
 def dft_table(bins, feeds_per):

time: 86.9 us -> 86.9 us (level)
  waiting for transfers between devices: 21.4 us -> 18.1 us
  blocking collectives: 40.8 us -> 43.3 us
    all_to_all x1, waiting for transfers between devices: 21.4 us -> 18.1 us  [body(): lax.all_to_all(calibrated, 'wide', split_axis=0, concat_axis=0, axis_inde...]
    all_to_all x1, blocking collectives: 40.8 us -> 43.3 us  [body(): lax.all_to_all(power, ('wide', 'pol'), split_axis=0, concat_axis=0, axis_...]
where the time goes in v2:
time: 86.9 us; the launch traced here: 86.6 us
  blocking collectives  43.3 us (50%)
  waiting for transfers between devices  18.1 us (21%)
  Pallas kernels  11.3 us (13%)
  starting transfers between devices  11 us (13%)
  other arithmetic  2.56 us (3%)
    all_to_all x1, blocking collectives, body(): lax.all_to_all(power, ('wide', 'pol'), split_axis=0, concat_axis=0, axis_...  43.3 us
    all_to_all x1, waiting for transfers between devices, body(): lax.all_to_all(calibrated, 'wide', split_axis=0, concat_axis=0, axis_inde...  18.1 us
    all_to_all x1, starting transfers between devices, body(): lax.all_to_all(calibrated, 'wide', split_axis=0, concat_axis=0, axis_inde...  11 us
    pallas_call x1, Pallas kernels, route(): pl.pallas_call(route_kernel, out_shape=(jax.ShapeDtypeStruct((groups, siz...  4.32 us
    pallas_call x1, Pallas kernels, calibrate(): pl.pallas_call(calibrate_kernel, out_shape=jax.ShapeDtypeStruct((channels...  3.21 us
    pallas_call x1, Pallas kernels, form_beams(): pl.pallas_call(beams_kernel, out_shape=jax.ShapeDtypeStruct((feeds_total...  2.92 us
    convert_element_type x1, other arithmetic, dft_table(): cos_table = jnp.cos(theta).astype(jnp.bfloat16)  2.5 us
  transfers between devices with their start and end apart: 1, of which 1 were waited for; matrix products, arithmetic and copies ran while one was open for 3% of the time, Pallas kernels for 5%

profile of v2, /device:TPU:1, one launch (start us, length us, event | category | flops | bytes accessed | tf_op | source)
XLA Modules:
  0.0 86.6 jit_solution(2284552074687985235)
XLA Ops:
  0.0 3.2 %calibrate.1 = bf16[64,2,2,16,256]{4,3,2,1,0:T(8,128)(2,1)} custom-call(bf16[2,1,16,128,256]{4,3,2,1,0:T(8,128)(2,1)} %volts_ref.1, f32[2,2,16,128]{3,2,1,0:T(8,128)} %gains_ref.1), custom_call_target="tpu_custom_call" | custom-call | flops 536870912 | bytes 4194304 | tf_op jit(solution)/shard_map/calibrate/pallas_call | solution.py:83
  3.2 0.0 copy-start
  3.2 0.0 copy-start.1
  3.2 11.0 %all-to-all-start = ((bf16[64,2,2,16,256]{4,3,2,1,0:T(8,128)(2,1)}), bf16[64,2,2,16,256]{4,3,2,1,0:T(8,128)(2,1)S(1)}, u32[]{:S(2)}, u32[]{:S(2)}) async-start(bf16[64,2,2,16,256]{4,3,2,1,0:T(8,128)(2,1)} %calibrate.1), calls=%async_computation | async-start | bytes 4194304 | tf_op jit(solution)/shard_map/all_to_all | solution.py:317
  14.3 0.0 copy-done
  14.4 0.0 copy-done.1
  14.4 2.5 %cosine_convert_fusion = (bf16[2,256,256]{2,1,0:T(8,128)(2,1)S(1)}, bf16[2,256,256]{2,1,0:T(8,128)(2,1)S(1)}) fusion(s32[2,256]{1,0:T(2,128)S(1)} %copy-done.1), kind=kLoop, calls=%fused_computation.8 | loop fusion | flops 2097152 | bytes 526336 | tf_op jit(solution)/shard_map/convert_element_type | solution.py:28
  16.9 0.2 broadcast_in_dim.2.lookup_ref
  17.1 4.3 %route.1 = (s32[4,256]{1,0:T(4,128)S(1)}, s32[256,128]{1,0:T(8,128)S(1)}, bf16[4,512,256]{2,1,0:T(8,128)(2,1)S(1)}, bf16[12,4,512,256]{3,2,1,0:T(8,128)(2,1)}) custom-call(s32[4,256]{1,0:T(4,128)S(1)} %reshape.5.rows_ref, s32[1024,128]{1,0:T(8,128)S(1)} %broadcast_in_dim.2.lookup_ref, bf16[2,512,256]{2,1,0:T(8,128)(2,1)S(1)} %pad_maximum_fusion.table_ref), custom_call_target="tpu_custom_call" | custom-call | flops 2147483648 | bytes 8388608 | tf_op jit(solution)/shard_map/route/pallas_call | solution.py:181
  21.4 18.1 %all-to-all-done.turned_ref = bf16[64,2,2,16,256]{4,3,2,1,0:T(8,128)(2,1)S(1)} async-done(((bf16[64,2,2,16,256]{4,3,2,1,0:T(8,128)(2,1)}), bf16[64,2,2,16,256]{4,3,2,1,0:T(8,128)(2,1)S(1)}, u32[]{:S(2)}, u32[]{:S(2)}) %all-to-all-start) | async-done | bytes 2097184 | tf_op jit(solution)/shard_map/all_to_all | solution.py:317
  39.6 2.9 %form_beams.1 = bf16[256,16,128]{2,1,0:T(8,128)(2,1)S(1)} custom-call(bf16[64,2,2,16,256]{4,3,2,1,0:T(8,128)(2,1)S(1)} %all-to-all-done.turned_ref, s32[4,256]{1,0:T(4,128)S(1)} %get-tuple-element.9.swap_ref, s32[256,128]{1,0:T(8,128)S(1)} %get-tuple-element.10.choice_ref, bf16[4,512,256]{2,1,0:T(8,128)(2,1)S(1)} %get-tuple-element.11.first_ref, ...), custom_call_target="tpu_custom_call" | custom-call | flops 1610612736 | bytes 8388608 | tf_op jit(solution)/shard_map/form_beams/pallas_call | solution.py:257
  42.5 43.3 %all_to_all.10.sent_ref = bf16[256,16,128]{2,1,0:T(8,128)(2,1)S(1)} all-to-all(bf16[256,16,128]{2,1,0:T(8,128)(2,1)S(1)} %form_beams.1), channel_id=1, replica_groups={{0,4,16,20,32,36,48,52,64,68,80,84,96,100,112,116,128,132,144,148,160,1..., dimensions={0} | all-to-all | bytes 2097152 | tf_op jit(solution)/shard_map/all_to_all | solution.py:327
  85.8 0.9 %add_streams.1 = f32[4,128,256]{2,1,0:T(8,128)} custom-call(bf16[256,16,128]{2,1,0:T(8,128)(2,1)S(1)} %all_to_all.10.sent_ref), custom_call_target="tpu_custom_call" | custom-call | flops 1048576 | bytes 2097152 | tf_op jit(solution)/shard_map/add_streams/pallas_call | solution.py:297
  (3 shorter events, 0.1 us)
Async XLA Ops:
  3.2 11.1 %copy-start = (s32[1024]{0:T(1024)S(1)}, s32[1024]{0:T(1024)}, u32[]{:S(2)}) copy-start(s32[1024]{0:T(1024)} %param.6) | copy-start | bytes 12292
  3.2 11.1 %copy-start.1 = (s32[2,256]{1,0:T(2,128)S(1)}, s32[2,256]{1,0:T(2,128)}, u32[]{:S(2)}) copy-start(s32[2,256]{1,0:T(2,128)} %param.7) | copy-start | bytes 6148
  3.2 36.3 %all-to-all-start = ((bf16[64,2,2,16,256]{4,3,2,1,0:T(8,128)(2,1)}), bf16[64,2,2,16,256]{4,3,2,1,0:T(8,128)(2,1)S(1)}, u32[]{:S(2)}, u32[]{:S(2)}) async-start(bf16[64,2,2,16,256]{4,3,2,1,0:T(8,128)(2,1)} %calibrate.1), calls=%async_computation | async-start | bytes 4194304 | tf_op jit(solution)/shard_map/all_to_all | solution.py:317

commit v3 on v1

--- a/solution.py
+++ b/solution.py
@@ -242,12 +242,9 @@
     swaps(0)
     zero = [field_of(0, first_ref, c) for c in range(cylinders)]
     swaps(1)
-    powers(0, zero, range(0, size // 2, 8))
     fetch.wait()
-    one = []
-    for c in range(cylinders):
-        one.append(field_of(1, second_buf, c))
-        powers(0, zero, range(size // 2 + c * size // 8, size // 2 + (c + 1) * size // 8, 8))
+    one = [field_of(1, second_buf, c) for c in range(cylinders)]
+    powers(0, zero, range(0, size, 8))
     powers(1, one, range(0, size, 8))
 
 

time: 86.9 us -> 86.9 us (level)
  no operation moved by 1% of the time
where the time goes in v3:
time: 86.9 us; the launch traced here: 86.7 us
  blocking collectives  40.8 us (47%)
  waiting for transfers between devices  21.4 us (25%)
  Pallas kernels  11.3 us (13%)
  starting transfers between devices  10.4 us (12%)
  other arithmetic  2.56 us (3%)
    all_to_all x1, blocking collectives, body(): lax.all_to_all(power, ('wide', 'pol'), split_axis=0, concat_axis=0, axis_...  40.8 us
    all_to_all x1, waiting for transfers between devices, body(): lax.all_to_all(calibrated, 'wide', split_axis=0, concat_axis=0, axis_inde...  21.4 us
    all_to_all x1, starting transfers between devices, body(): lax.all_to_all(calibrated, 'wide', split_axis=0, concat_axis=0, axis_inde...  10.4 us
    pallas_call x1, Pallas kernels, route(): pl.pallas_call(route_kernel, out_shape=(jax.ShapeDtypeStruct((groups, siz...  4.32 us
    pallas_call x1, Pallas kernels, calibrate(): pl.pallas_call(calibrate_kernel, out_shape=jax.ShapeDtypeStruct((channels...  3.21 us
    pallas_call x1, Pallas kernels, form_beams(): pl.pallas_call(beams_kernel, out_shape=jax.ShapeDtypeStruct((feeds_total...  2.93 us
    convert_element_type x1, other arithmetic, dft_table(): cos_table = jnp.cos(theta).astype(jnp.bfloat16)  2.5 us
  transfers between devices with their start and end apart: 1, of which 1 were waited for; matrix products, arithmetic and copies ran while one was open for 3% of the time, Pallas kernels for 5%

profile of v3, /device:TPU:1, one launch (start us, length us, event | category | flops | bytes accessed | tf_op | source)
XLA Modules:
  0.0 86.7 jit_solution(8361334468166351366)
XLA Ops:
  0.0 3.2 %calibrate.1 = bf16[64,2,2,16,256]{4,3,2,1,0:T(8,128)(2,1)} custom-call(bf16[2,1,16,128,256]{4,3,2,1,0:T(8,128)(2,1)} %volts_ref.1, f32[2,2,16,128]{3,2,1,0:T(8,128)} %gains_ref.1), custom_call_target="tpu_custom_call" | custom-call | flops 536870912 | bytes 4194304 | tf_op jit(solution)/shard_map/calibrate/pallas_call | solution.py:83
  3.2 0.0 copy-start
  3.2 0.0 copy-start.1
  3.2 10.4 %all-to-all-start = ((bf16[64,2,2,16,256]{4,3,2,1,0:T(8,128)(2,1)}), bf16[64,2,2,16,256]{4,3,2,1,0:T(8,128)(2,1)S(1)}, u32[]{:S(2)}, u32[]{:S(2)}) async-start(bf16[64,2,2,16,256]{4,3,2,1,0:T(8,128)(2,1)} %calibrate.1), calls=%async_computation | async-start | bytes 4194304 | tf_op jit(solution)/shard_map/all_to_all | solution.py:314
  13.6 0.0 copy-done
  13.7 0.0 copy-done.1
  13.7 2.5 %cosine_convert_fusion = (bf16[2,256,256]{2,1,0:T(8,128)(2,1)S(1)}, bf16[2,256,256]{2,1,0:T(8,128)(2,1)S(1)}) fusion(s32[2,256]{1,0:T(2,128)S(1)} %copy-done.1), kind=kLoop, calls=%fused_computation.8 | loop fusion | flops 2097152 | bytes 526336 | tf_op jit(solution)/shard_map/convert_element_type | solution.py:28
  16.2 0.2 broadcast_in_dim.2.lookup_ref
  16.4 4.3 %route.1 = (s32[4,256]{1,0:T(4,128)S(1)}, s32[256,128]{1,0:T(8,128)S(1)}, bf16[4,512,256]{2,1,0:T(8,128)(2,1)S(1)}, bf16[12,4,512,256]{3,2,1,0:T(8,128)(2,1)}) custom-call(s32[4,256]{1,0:T(4,128)S(1)} %reshape.5.rows_ref, s32[1024,128]{1,0:T(8,128)S(1)} %broadcast_in_dim.2.lookup_ref, bf16[2,512,256]{2,1,0:T(8,128)(2,1)S(1)} %pad_maximum_fusion.table_ref), custom_call_target="tpu_custom_call" | custom-call | flops 2147483648 | bytes 8388608 | tf_op jit(solution)/shard_map/route/pallas_call | solution.py:181
  20.7 21.4 %all-to-all-done.turned_ref = bf16[64,2,2,16,256]{4,3,2,1,0:T(8,128)(2,1)S(1)} async-done(((bf16[64,2,2,16,256]{4,3,2,1,0:T(8,128)(2,1)}), bf16[64,2,2,16,256]{4,3,2,1,0:T(8,128)(2,1)S(1)}, u32[]{:S(2)}, u32[]{:S(2)}) %all-to-all-start) | async-done | bytes 2097184 | tf_op jit(solution)/shard_map/all_to_all | solution.py:314
  42.1 2.9 %form_beams.1 = bf16[256,16,128]{2,1,0:T(8,128)(2,1)S(1)} custom-call(bf16[64,2,2,16,256]{4,3,2,1,0:T(8,128)(2,1)S(1)} %all-to-all-done.turned_ref, s32[4,256]{1,0:T(4,128)S(1)} %get-tuple-element.9.swap_ref, s32[256,128]{1,0:T(8,128)S(1)} %get-tuple-element.10.choice_ref, bf16[4,512,256]{2,1,0:T(8,128)(2,1)S(1)} %get-tuple-element.11.first_ref, ...), custom_call_target="tpu_custom_call" | custom-call | flops 1610612736 | bytes 8388608 | tf_op jit(solution)/shard_map/form_beams/pallas_call | solution.py:254
  45.1 40.8 %all_to_all.10.sent_ref = bf16[256,16,128]{2,1,0:T(8,128)(2,1)S(1)} all-to-all(bf16[256,16,128]{2,1,0:T(8,128)(2,1)S(1)} %form_beams.1), channel_id=1, replica_groups={{0,4,16,20,32,36,48,52,64,68,80,84,96,100,112,116,128,132,144,148,160,1..., dimensions={0} | all-to-all | bytes 2097152 | tf_op jit(solution)/shard_map/all_to_all | solution.py:324
  85.8 0.9 %add_streams.1 = f32[4,128,256]{2,1,0:T(8,128)} custom-call(bf16[256,16,128]{2,1,0:T(8,128)(2,1)S(1)} %all_to_all.10.sent_ref), custom_call_target="tpu_custom_call" | custom-call | flops 1048576 | bytes 2097152 | tf_op jit(solution)/shard_map/add_streams/pallas_call | solution.py:294
  (3 shorter events, 0.1 us)
Async XLA Ops:
  3.2 10.4 %copy-start = (s32[1024]{0:T(1024)S(1)}, s32[1024]{0:T(1024)}, u32[]{:S(2)}) copy-start(s32[1024]{0:T(1024)} %param.6) | copy-start | bytes 12292
  3.2 10.4 %copy-start.1 = (s32[2,256]{1,0:T(2,128)S(1)}, s32[2,256]{1,0:T(2,128)}, u32[]{:S(2)}) copy-start(s32[2,256]{1,0:T(2,128)} %param.7) | copy-start | bytes 6148
  3.2 38.9 %all-to-all-start = ((bf16[64,2,2,16,256]{4,3,2,1,0:T(8,128)(2,1)}), bf16[64,2,2,16,256]{4,3,2,1,0:T(8,128)(2,1)S(1)}, u32[]{:S(2)}, u32[]{:S(2)}) async-start(bf16[64,2,2,16,256]{4,3,2,1,0:T(8,128)(2,1)} %calibrate.1), calls=%async_computation | async-start | bytes 4194304 | tf_op jit(solution)/shard_map/all_to_all | solution.py:314
